TPU v7x, 32 devices: a whole 2x2x4 slice. The times are simulated.
32 devices in a mesh: ctx: 16 (over z, x, core), tp: 2 (over y).
Axes of the slice: x: 2, y: 2, z: 4, core: 2. Of those that a mesh axis runs over, the one named last changes fastest.
Arguments:
- q_in: float32 [8192, 2048], P('ctx', 'tp'), may hold values from -6 to 6
- k_in: float32 [8192, 2048], P('ctx', 'tp'), may hold values from -6 to 6
- v_in: float32 [8192, 2048], P('ctx', 'tp'), may hold values from -6 to 6
- short_taps: float32 [3, 3, 2048], P(None, None, 'tp'), may hold values from -3.5 to 3.5
- long_filter: float32 [8192, 2048], P('ctx', 'tp'), may hold values from -6 to 6
- skip_gain: float32 [2048], P('tp'), may hold values from 0.5 to 1.5
- conv_saved: float32 [8192, 2048], P('ctx', 'tp'), may hold values from -6 to 6
- grad_out: float32 [8192, 2048], P('ctx', 'tp'), may hold values from -6 to 6
Outputs:
- grad_q: float32 [8192, 2048], P('ctx', 'tp')
- grad_k: float32 [8192, 2048], P('ctx', 'tp')
- grad_v: float32 [8192, 2048], P('ctx', 'tp')
- grad_filter: float32 [2048, 8192], P(('ctx', 'tp'))
- grad_taps: float32 [3, 3, 2048], P(None, None, 'tp')
- grad_skip: float32 [2048], P('tp')
All inputs are finite; a program needn't handle non-finite values.
Results may differ from a plain program's by a relative error of at most 0.00018.
Values sent between devices are 32-bit elements; how exact they have to be, the bound alone decides.
A program may use at most 128 MiB of HBM per device.

v0:
```python
import math

import jax
import jax.numpy as jnp
from jax import lax
from jax.sharding import PartitionSpec as P

highest = lax.Precision.HIGHEST


def passed_along(value, axis, steps):
    count = lax.axis_size(axis)
    leading, last = (max(0, -steps), min(count, count - steps))
    return lax.ppermute(value, axis, [(source, source + steps) for source in range(leading, last)])


def phase_table(index_product, modulus, direction):
    reduced = jnp.mod(index_product, modulus).astype(jnp.float32)
    radians = direction * 2.0 * math.pi / modulus * reduced
    return (jnp.cos(radians), jnp.sin(radians))


def complex_mul(left_real, left_imag, right_real, right_imag):
    return (
        left_real * right_real - left_imag * right_imag,
        left_real * right_imag + left_imag * right_real,
    )


def matmul_complex(form, table_cos, table_sin, data_real, data_imag):
    real_out = jnp.einsum(form, table_cos, data_real, precision=highest) - jnp.einsum(
        form, table_sin, data_imag, precision=highest
    )
    imag_out = jnp.einsum(form, table_cos, data_imag, precision=highest) + jnp.einsum(
        form, table_sin, data_real, precision=highest
    )
    return (real_out, imag_out)


def channel_correlate(filter_real, filter_imag, grad_w, ctx_count):
    local_rows = filter_real.shape[0]
    slab_width = filter_real.shape[1]
    group_width = slab_width // ctx_count
    seq_total = local_rows * ctx_count
    arrived = (
        lax.all_to_all(filter_real, "ctx", split_axis=1, concat_axis=0, tiled=True),
        lax.all_to_all(filter_imag, "ctx", split_axis=1, concat_axis=0, tiled=True),
        lax.all_to_all(grad_w, "ctx", split_axis=1, concat_axis=0, tiled=True),
    )
    block_shape = (ctx_count, local_rows, group_width)
    whole_real = arrived[0].reshape(block_shape)
    whole_imag = arrived[1].reshape(block_shape)
    whole_grad = arrived[2].reshape(block_shape)
    spectral_index = lax.iota(jnp.int32, 2 * ctx_count)
    device_index = lax.iota(jnp.int32, ctx_count)
    position = lax.iota(jnp.int32, local_rows)
    outer_cos, outer_sin = phase_table(
        spectral_index[:, None] * device_index[None, :], 2 * ctx_count, -1.0
    )
    filter_pair = matmul_complex("qd,djc->qjc", outer_cos, outer_sin, whole_real, whole_imag)
    grad_pair = (
        jnp.einsum("qd,djc->qjc", outer_cos, whole_grad, precision=highest),
        jnp.einsum("qd,djc->qjc", outer_sin, whole_grad, precision=highest),
    )
    twist_cos, twist_sin = phase_table(
        spectral_index[:, None] * position[None, :], 2 * seq_total, -1.0
    )
    filter_pair = complex_mul(
        filter_pair[0], filter_pair[1], twist_cos[:, :, None], twist_sin[:, :, None]
    )
    grad_pair = complex_mul(
        grad_pair[0], grad_pair[1], twist_cos[:, :, None], twist_sin[:, :, None]
    )
    inner_cos, inner_sin = phase_table(position[:, None] * position[None, :], local_rows, -1.0)
    filter_spec = matmul_complex(
        "jb,qjc->qbc", inner_cos, inner_sin, filter_pair[0], filter_pair[1]
    )
    grad_spec = matmul_complex("jb,qjc->qbc", inner_cos, inner_sin, grad_pair[0], grad_pair[1])
    product_real = filter_spec[0] * grad_spec[0] + filter_spec[1] * grad_spec[1]
    product_imag = filter_spec[0] * grad_spec[1] - filter_spec[1] * grad_spec[0]
    back_cos, back_sin = phase_table(position[:, None] * position[None, :], local_rows, 1.0)
    summed = matmul_complex("jb,qbc->qjc", back_cos, back_sin, product_real, product_imag)
    untwist_cos, untwist_sin = phase_table(
        spectral_index[:, None] * position[None, :], 2 * seq_total, 1.0
    )
    summed = complex_mul(summed[0], summed[1], untwist_cos[:, :, None], untwist_sin[:, :, None])
    final_cos, final_sin = phase_table(
        device_index[:, None] * spectral_index[None, :], 2 * ctx_count, 1.0
    )
    result = matmul_complex("dq,qjc->djc", final_cos, final_sin, summed[0], summed[1])
    factor = 1.0 / (2.0 * seq_total)
    flat_shape = (seq_total, group_width)
    returned = (
        lax.all_to_all(
            (result[0] * factor).reshape(flat_shape), "ctx", split_axis=0, concat_axis=1, tiled=True
        ),
        lax.all_to_all(
            (result[1] * factor).reshape(flat_shape), "ctx", split_axis=0, concat_axis=1, tiled=True
        ),
    )
    return (returned[0], returned[1])


def on_device(q_in, k_in, v_in, short_taps, long_filter, skip_gain, conv_saved, grad_out):
    local_rows = q_in.shape[0]
    slab_width = q_in.shape[1]
    ctx_count = lax.axis_size("ctx")
    tp_count = lax.axis_size("tp")
    seq_total = local_rows * ctx_count
    filter_scale = 1.0 / math.sqrt(seq_total)
    inputs = jnp.stack([q_in, k_in, v_in])
    previous = passed_along(inputs[:, local_rows - 2 :], "ctx", 1)
    extended = jnp.concatenate([previous, inputs], axis=1)
    first_tap = short_taps[:, 0][:, None, :]
    second_tap = short_taps[:, 1][:, None, :]
    third_tap = short_taps[:, 2][:, None, :]
    shorted = (
        first_tap * extended[:, 2:]
        + second_tap * extended[:, 1 : local_rows + 1]
        + third_tap * extended[:, :local_rows]
    )
    q_short = shorted[0]
    k_short = shorted[1]
    v_short = shorted[2]
    product_kv = k_short * v_short
    grad_w = grad_out * q_short
    grad_qs = grad_out * conv_saved
    corr_real, corr_imag = channel_correlate(long_filter, product_kv, grad_w, ctx_count)
    grad_z = skip_gain * grad_w + filter_scale * corr_real
    grad_long = -filter_scale * corr_imag
    grad_ks = grad_z * v_short
    grad_vs = grad_z * k_short
    grad_stack = jnp.stack([grad_qs, grad_ks, grad_vs])
    following = passed_along(grad_stack[:, :2], "ctx", -1)
    ext_grads = jnp.concatenate([grad_stack, following], axis=1)
    grad_inputs = (
        first_tap * ext_grads[:, :local_rows]
        + second_tap * ext_grads[:, 1 : local_rows + 1]
        + third_tap * ext_grads[:, 2:]
    )
    short_part = jnp.stack(
        [
            jnp.sum(grad_stack * extended[:, 2 - offset : 2 - offset + local_rows], axis=1)
            for offset in range(3)
        ],
        axis=1,
    )
    skip_part = jnp.sum(grad_w * product_kv, axis=0)
    short_total, skip_total = lax.psum((short_part, skip_part), "ctx")
    group_width = slab_width // ctx_count
    repeat = ctx_count // tp_count
    flipped = jnp.transpose(grad_long).reshape(repeat, tp_count * group_width, local_rows)
    settled = lax.all_to_all(
        lax.all_to_all(flipped, "tp", split_axis=1, concat_axis=0, tiled=True),
        "ctx",
        split_axis=0,
        concat_axis=2,
        tiled=True,
    )
    grad_filter = settled.reshape(group_width, seq_total)
    return (grad_inputs[0], grad_inputs[1], grad_inputs[2], grad_filter, short_total, skip_total)


def solution(mesh):
    placed = (
        P("ctx", "tp"),
        P("ctx", "tp"),
        P("ctx", "tp"),
        P(None, None, "tp"),
        P("ctx", "tp"),
        P("tp"),
        P("ctx", "tp"),
        P("ctx", "tp"),
    )
    return jax.shard_map(
        on_device,
        mesh=mesh,
        in_specs=placed,
        out_specs=(
            P("ctx", "tp"),
            P("ctx", "tp"),
            P("ctx", "tp"),
            P(("ctx", "tp"), None),
            P(None, None, "tp"),
            P("tp"),
        ),
        check_vma=False,
    )
```

profile of v0, /device:TPU:0, one launch (start us, length us, event | category | flops | bytes accessed | tf_op | source)
XLA Modules:
  0.0 653.7 jit_solution(9248305249271942225)
XLA Ops:
  0.6 2.9 copy.121
  3.5 7.4 %all-to-all-start = ((f32[512,16,64]{0,2,1:T(8,128)}), f32[512,16,64]{0,2,1:T(8,128)}, u32[]{:S(2)}, u32[]{:S(2)}) async-start(f32[512,16,64]{0,2,1:T(8,128)} %bitcast.7), calls=%async_computation | async-start | bytes 4194304 | tf_op jit(solution)/shard_map/all_to_all | solution.py:46
  10.9 1.9 copy.115
  12.9 2.9 copy.116
  15.8 2.9 copy.117
  18.6 2.9 pad_maximum_fusion.1
  23.2 1.9 copy.118
  25.1 2.3 collective-permute-start
  28.2 1.7 copy.119
  29.8 5.5 maximum_maximum_fusion
  35.4 4.0 multiply_add_fusion
  39.4 2.7 copy-done.1
  42.1 1.8 slice_multiply_fusion.2
  43.9 8.2 %all-to-all-done = f32[512,16,64]{0,2,1:T(8,128)} async-done(((f32[512,16,64]{0,2,1:T(8,128)}), f32[512,16,64]{0,2,1:T(8,128)}, u32[]{:S(2)}, u32[]{:S(2)}) %all-to-all-start) | async-done | bytes 2097184 | tf_op jit(solution)/shard_map/all_to_all | solution.py:46
  52.1 26.5 %all-to-all-start.1 = ((f32[512,16,64]{0,2,1:T(8,128)}), f32[512,16,64]{0,2,1:T(8,128)}, u32[]{:S(2)}, u32[]{:S(2)}) async-start(f32[512,16,64]{0,2,1:T(8,128)} %bitcast.182), calls=%async_computation.1 | async-start | bytes 4194304 | tf_op jit(solution)/shard_map/all_to_all | solution.py:47
  78.6 2.9 copy.114
  81.5 2.9 copy.113
  84.4 6.6 %fusion.55 = (f32[1024]{0:T(1024)S(1)}, f32[512,1024]{0,1:T(8,128)}, f32[1,512,1024]{1,2,0:T(8,128)}) fusion(f32[3,512,1024]{1,2,0:T(8,128)} %copy-done.1, f32[512,1024]{0,1:T(8,128)} %copy.113, f32[512,1024]{0,1:T(8,128)} %copy.114), kind=kLoop, calls=%fused_computation.70 | loop fusion | flops 2620416 | bytes 14684160 | tf_op jit(solution)/shard_map/reduce_sum | solution.py:148
  91.0 28.8 %all-to-all-done.1 = f32[512,16,64]{0,2,1:T(8,128)} async-done(((f32[512,16,64]{0,2,1:T(8,128)}), f32[512,16,64]{0,2,1:T(8,128)}, u32[]{:S(2)}, u32[]{:S(2)}) %all-to-all-start.1) | async-done | bytes 2097184 | tf_op jit(solution)/shard_map/all_to_all | solution.py:47
  119.8 11.5 %all-to-all-start.2 = ((f32[512,16,64]{0,2,1:T(8,128)}), f32[512,16,64]{0,2,1:T(8,128)}, u32[]{:S(2)}, u32[]{:S(2)}) async-start(f32[512,16,64]{0,2,1:T(8,128)} %bitcast.181), calls=%async_computation.2 | async-start | bytes 4194304 | tf_op jit(solution)/shard_map/all_to_all | solution.py:48
  131.8 6.0 fusion.65
  137.9 6.0 fusion.61
  143.9 7.5 %convolution_subtract_fusion = f32[32,512,64]{1,0,2:T(8,128)} fusion(f32[32,512,64]{1,0,2:T(8,128)S(1)} %fusion.65, f32[512,16,64]{0,2,1:T(8,128)} %all-to-all-done.1), kind=kOutput, calls=%fused_computation.53 | convolution fusion | flops 202382336 | bytes 10485760 | tf_op jit(solution)/shard_map/qd,djc->qjc/dot_general | solution.py:31
  151.4 7.9 %convolution_add_fusion = f32[32,512,64]{1,0,2:T(8,128)} fusion(f32[32,512,64]{1,0,2:T(8,128)S(1)} %fusion.61, f32[512,16,64]{0,2,1:T(8,128)} %all-to-all-done), kind=kOutput, calls=%fused_computation.52 | convolution fusion | flops 202382336 | bytes 10485760 | tf_op jit(solution)/shard_map/qd,djc->qjc/dot_general | solution.py:34
  159.3 13.1 %all-to-all-done.2 = f32[512,16,64]{0,2,1:T(8,128)} async-done(((f32[512,16,64]{0,2,1:T(8,128)}), f32[512,16,64]{0,2,1:T(8,128)}, u32[]{:S(2)}, u32[]{:S(2)}) %all-to-all-start.2) | async-done | bytes 2097184 | tf_op jit(solution)/shard_map/all_to_all | solution.py:48
  172.4 7.4 %fusion.59 = f32[32,512,64]{1,0,2:T(8,128)} fusion(f32[512,16,64]{0,2,1:T(8,128)} %all-to-all-done.2), kind=kOutput, calls=%fused_computation.75 | convolution fusion | flops 201333760 | bytes 6291456 | tf_op jit(solution)/shard_map/qd,djc->qjc/dot_general | solution.py:62
  179.9 10.1 %multiply_subtract_fusion.1 = (f32[32,512,64]{1,0,2:T(8,128)S(1)}, f32[32,512,64]{1,0,2:T(8,128)S(1)}, f32[32,512,64]{1,0,2:T(8,128)S(1)}, f32[32,512,64]{1,0,2:T(8,128)S(1)}) fusion(f32[32,512,64]{1,0,2:T(8,128)} %fusion.59, f32[32,512]{1,0:T(8,128)S(1)} %get-tuple-element.59, f32[32,512]{1,0:T(8,128)S(1)} %get-tuple-element.60, ...), kind=kOutput, calls=%fused_computation.25 | convolution fusion | flops 213916672 | bytes 31588352 | tf_op jit(solution)/shard_map/qd,djc->qjc/dot_general | solution.py:63
  190.0 12.6 %fusion.18 = f32[32,64,512]{2,1,0:T(8,128)S(1)} fusion(f32[32,512,64]{1,0,2:T(8,128)S(1)} %get-tuple-element.44), kind=kOutput, calls=%fused_computation.36 | convolution fusion | flops 6446120960 | bytes 8388608 | tf_op jit(solution)/shard_map/jb,qjc->qbc/dot_general | solution.py:34
  202.6 12.8 %fusion.20 = f32[32,64,512]{2,1,0:T(8,128)S(1)} fusion(f32[32,512,64]{1,0,2:T(8,128)S(1)} %get-tuple-element.44), kind=kOutput, calls=%fused_computation.38 | convolution fusion | flops 6446120960 | bytes 8388608 | tf_op jit(solution)/shard_map/jb,qjc->qbc/dot_general | solution.py:31
  215.5 15.8 %fusion.26 = f32[32,64,512]{2,1,0:T(8,128)} fusion(f32[32,512,64]{1,0,2:T(8,128)S(1)} %get-tuple-element.52), kind=kOutput, calls=%fused_computation.44 | convolution fusion | flops 6446120960 | bytes 8388608 | tf_op jit(solution)/shard_map/jb,qjc->qbc/dot_general | solution.py:34
  231.3 12.7 %fusion.28 = f32[32,64,512]{2,1,0:T(8,128)S(1)} fusion(f32[32,512,64]{1,0,2:T(8,128)S(1)} %get-tuple-element.52), kind=kOutput, calls=%fused_computation.46 | convolution fusion | flops 6446120960 | bytes 8388608 | tf_op jit(solution)/shard_map/jb,qjc->qbc/dot_general | solution.py:31
  244.0 13.4 %fusion.40 = f32[32,64,512]{2,1,0:T(8,128)S(1)} fusion(f32[32,64,512]{2,1,0:T(8,128)S(1)} %fusion.20, f32[32,512,64]{1,0,2:T(8,128)S(1)} %get-tuple-element.43), kind=kOutput, calls=%fused_computation.56 | convolution fusion | flops 6447169536 | bytes 12582912 | tf_op jit(solution)/shard_map/jb,qjc->qbc/dot_general | solution.py:31
  257.3 15.8 %fusion.43 = f32[32,64,512]{2,1,0:T(8,128)} fusion(f32[32,64,512]{2,1,0:T(8,128)S(1)} %fusion.18, f32[32,512,64]{1,0,2:T(8,128)S(1)} %get-tuple-element.43), kind=kOutput, calls=%fused_computation.57 | convolution fusion | flops 6447169536 | bytes 12582912 | tf_op jit(solution)/shard_map/jb,qjc->qbc/dot_general | solution.py:34
  273.2 15.9 %fusion.34 = f32[32,64,512]{2,1,0:T(8,128)} fusion(f32[32,64,512]{2,1,0:T(8,128)S(1)} %fusion.28, f32[32,512,64]{1,0,2:T(8,128)S(1)} %get-tuple-element.53), kind=kOutput, calls=%fused_computation.54 | convolution fusion | flops 6447169536 | bytes 12582912 | tf_op jit(solution)/shard_map/jb,qjc->qbc/dot_general | solution.py:31
  289.1 22.2 %multiply_add_fusion.1 = (f32[32,64,512]{2,1,0:T(8,128)S(1)}, f32[32,64,512]{2,1,0:T(8,128)S(1)}) fusion(f32[32,64,512]{2,1,0:T(8,128)} %fusion.43, f32[32,64,512]{2,1,0:T(8,128)} %fusion.34, f32[32,64,512]{2,1,0:T(8,128)S(1)} %fusion.40, f32[32,64,512]{2,1,0:T(8,128)} %fusion.26, f32[32,512,64]{1,0,2:T(8,128)S(1)} %get-tuple-element.53), kind=kOutput, calls=%fused_computation.23 | convolution fusion | flops 6453460992 | bytes 29360128 | tf_op jit(solution)/shard_map/jb,qjc->qbc/dot_general | solution.py:34
  311.3 11.2 %fusion.2 = f32[32,64,512]{2,1,0:T(8,128)S(1)} fusion(f32[32,64,512]{2,1,0:T(8,128)S(1)} %get-tuple-element.38), kind=kOutput, calls=%fused_computation.12 | convolution fusion | flops 6446120960 | bytes 8388608 | tf_op jit(solution)/shard_map/jb,qbc->qjc/dot_general | solution.py:34
  322.5 10.8 %fusion.4 = f32[32,64,512]{2,1,0:T(8,128)S(1)} fusion(f32[32,64,512]{2,1,0:T(8,128)S(1)} %get-tuple-element.38), kind=kOutput, calls=%fused_computation.14 | convolution fusion | flops 6446120960 | bytes 8388608 | tf_op jit(solution)/shard_map/jb,qbc->qjc/dot_general | solution.py:31
  333.3 11.8 %fusion.46 = f32[32,64,512]{2,1,0:T(8,128)S(1)} fusion(f32[32,64,512]{2,1,0:T(8,128)S(1)} %fusion.4, f32[32,64,512]{2,1,0:T(8,128)S(1)} %get-tuple-element.37), kind=kOutput, calls=%fused_computation.58 | convolution fusion | flops 6447169536 | bytes 12582912 | tf_op jit(solution)/shard_map/jb,qbc->qjc/dot_general | solution.py:31
  345.1 15.2 %subtract_bitcast_fusion = (f32[32,512,64]{1,2,0:T(8,128)S(1)}, f32[32,512,64]{1,2,0:T(8,128)S(1)}) fusion(f32[32,64,512]{2,1,0:T(8,128)S(1)} %fusion.46, f32[32,512]{1,0:T(8,128)S(1)} %get-tuple-element.61, f32[32,512]{1,0:T(8,128)S(1)} %get-tuple-element.62, f32[32,64,512]{2,1,0:T(8,128)S(1)} %fusion.2, f32[32,64,512]{2,1,0:T(8,128)S(1)} %get-tuple-element.37), kind=kOutput, calls=%fused_computation.21 | convolution fusion | flops 6453460992 | bytes 21102592 | tf_op jit(solution)/shard_map/jb,qbc->qjc/dot_general | solution.py:34
  360.3 4.4 fusion.10
  364.7 4.6 add_multiply_fusion
  370.5 58.5 %all_to_all.98 = f32[16,512,64]{1,2,0:T(8,128)S(1)} all-to-all(f32[16,512,64]{1,2,0:T(8,128)S(1)} %copy.140), channel_id=1, replica_groups=mesh['ctx'=16,'tp'=2] {'ctx'}, dimensions={0} | all-to-all | bytes 4194304 | tf_op jit(solution)/shard_map/all_to_all | solution.py:97
  429.4 2.6 copy.141
  432.0 4.8 all-to-all-start.5
  436.8 7.0 %fusion.12 = f32[16,512,64]{1,0,2:T(8,128)S(1)} fusion(f32[32,512,64]{1,2,0:T(8,128)} %copy-done.8), kind=kOutput, calls=%fused_computation.30 | convolution fusion | flops 201333760 | bytes 6291456 | tf_op jit(solution)/shard_map/dq,qjc->djc/dot_general | solution.py:31
  443.8 4.6 subtract_multiply_fusion
  448.4 2.6 copy.135
  451.0 12.0 %all-to-all-done.5 = f32[8,128,512]{2,0,1:T(8,128)} async-done(((f32[8,128,512]{2,0,1:T(8,128)}), f32[8,128,512]{2,0,1:T(8,128)}, u32[]{:S(2)}, u32[]{:S(2)}) %all-to-all-start.5) | async-done | bytes 2097184 | tf_op jit(solution)/shard_map/all_to_all | solution.py:154
  462.9 4.9 all-to-all-start.3
  467.9 4.2 copy.143
  472.0 37.0 %all-to-all-done.3 = f32[16,512,64]{1,2,0:T(8,128)} async-done(((f32[16,512,64]{1,2,0:T(8,128)}), f32[16,512,64]{1,2,0:T(8,128)}, u32[]{:S(2)}, u32[]{:S(2)}) %all-to-all-start.3) | async-done | bytes 2097184 | tf_op jit(solution)/shard_map/all_to_all | solution.py:94
  509.0 11.4 %all-to-all-start.6 = ((f32[16,64,512]{2,1,0:T(8,128)}), f32[16,64,512]{2,1,0:T(8,128)}, u32[]{:S(2)}, u32[]{:S(2)}) async-start(f32[16,64,512]{2,1,0:T(8,128)} %bitcast.183), calls=%async_computation.6 | async-start | bytes 4194304 | tf_op jit(solution)/shard_map/all_to_all | solution.py:153
  520.4 2.0 broadcast_multiply_fusion.1
  522.6 2.9 fusion.56
  528.9 1.9 copy.136
  532.1 1.8 collective-permute-done.1
  535.6 3.8 pad_maximum_fusion
  541.9 12.6 %multiply_reduce_fusion.1 = (f32[3,1024]{1,0:T(4,128)S(1)}, f32[3,1024]{1,0:T(4,128)S(1)}, f32[3,1024]{1,0:T(4,128)S(1)}, f32[3,512,1024]{1,2,0:T(8,128)}) fusion(f32[3,514,1024]{1,2,0:T(8,128)} %copy-done, f32[1,512,1024]{1,2,0:T(8,128)S(1)} %copy-done.14, f32[1,512,1024]{1,2,0:T(8,128)S(1)} %copy-done.12, f32[1,512,1024]{1,2,0:T(8,128)S(1)} %copy-done.10, ...), kind=kLoop, calls=%fused_computation.9 | loop fusion | flops 23583744 | bytes 44113920 | tf_op jit(solution)/shard_map/reduce_sum | solution.py:143
  554.6 81.7 %all-reduce = (f32[3,3,1024]{2,0,1:T(4,128)S(1)}, f32[1024]{0:T(1024)}) all-reduce(f32[3,3,1024]{2,0,1:T(4,128)S(1)} %pad_maximum_fusion.3, f32[1024]{0:T(1024)S(1)} %get-tuple-element.35), channel_id=1, replica_groups=mesh['ctx'=16,'tp'=2] {'ctx'}, use_global_device_ids=true, to_apply=%region_3.4 | all-reduce | flops 10240 | bytes 81920 | tf_op jit(solution)/shard_map/psum | solution.py:149
  637.0 5.6 slice_bitcast_fusion
  642.5 2.9 copy.147
  645.4 2.9 copy.146
  648.3 1.8 copy.145
  650.1 3.1 copy.153
  (51 shorter events, 14.2 us)
Async XLA Ops:
  3.5 48.6 %all-to-all-start = ((f32[512,16,64]{0,2,1:T(8,128)}), f32[512,16,64]{0,2,1:T(8,128)}, u32[]{:S(2)}, u32[]{:S(2)}) async-start(f32[512,16,64]{0,2,1:T(8,128)} %bitcast.7), calls=%async_computation | async-start | bytes 4194304 | tf_op jit(solution)/shard_map/all_to_all | solution.py:46
  21.6 5.8 copy-start.16
  25.1 3.1 collective-permute-start
  29.8 5.5 copy-start.2
  29.8 5.5 copy-start.4
  35.4 4.0 copy-start
  39.4 2.7 copy-start.1
  52.1 67.7 %all-to-all-start.1 = ((f32[512,16,64]{0,2,1:T(8,128)}), f32[512,16,64]{0,2,1:T(8,128)}, u32[]{:S(2)}, u32[]{:S(2)}) async-start(f32[512,16,64]{0,2,1:T(8,128)} %bitcast.182), calls=%async_computation.1 | async-start | bytes 4194304 | tf_op jit(solution)/shard_map/all_to_all | solution.py:47
  119.8 52.6 %all-to-all-start.2 = ((f32[512,16,64]{0,2,1:T(8,128)}), f32[512,16,64]{0,2,1:T(8,128)}, u32[]{:S(2)}, u32[]{:S(2)}) async-start(f32[512,16,64]{0,2,1:T(8,128)} %bitcast.181), calls=%async_computation.2 | async-start | bytes 4194304 | tf_op jit(solution)/shard_map/all_to_all | solution.py:48
  360.3 9.0 %copy-start.6 = (f32[32,512,64]{1,2,0:T(8,128)}, f32[32,512,64]{1,2,0:T(8,128)S(1)}, u32[]{:S(2)}) copy-start(f32[32,512,64]{1,2,0:T(8,128)S(1)} %get-tuple-element.41) | copy-start | bytes 12582916
  360.3 9.0 %copy-start.8 = (f32[32,512,64]{1,2,0:T(8,128)}, f32[32,512,64]{1,2,0:T(8,128)S(1)}, u32[]{:S(2)}) copy-start(f32[32,512,64]{1,2,0:T(8,128)S(1)} %get-tuple-element.42) | copy-start | bytes 12582916
  432.0 31.0 %all-to-all-start.5 = ((f32[8,128,512]{2,0,1:T(8,128)}), f32[8,128,512]{2,0,1:T(8,128)}, u32[]{:S(2)}, u32[]{:S(2)}) async-start(f32[8,128,512]{2,0,1:T(8,128)} %copy.141), calls=%async_computation.5 | async-start | bytes 4194304 | tf_op jit(solution)/shard_map/all_to_all | solution.py:154
  436.8 7.0 %copy-start.7 = (f32[32,512,64]{1,2,0:T(8,128)S(1)}, f32[32,512,64]{1,2,0:T(8,128)}, u32[]{:S(2)}) copy-start(f32[32,512,64]{1,2,0:T(8,128)} %copy-done.6) | copy-start | bytes 12582916
  462.9 46.1 %all-to-all-start.3 = ((f32[16,512,64]{1,2,0:T(8,128)}), f32[16,512,64]{1,2,0:T(8,128)}, u32[]{:S(2)}, u32[]{:S(2)}) async-start(f32[16,512,64]{1,2,0:T(8,128)} %copy.135), calls=%async_computation.3 | async-start | bytes 4194304 | tf_op jit(solution)/shard_map/all_to_all | solution.py:94
  509.0 13.4 %copy-start.17 = (f32[1024]{0:T(1024)S(1)}, f32[1024]{0:T(1024)}, u32[]{:S(2)}) copy-start(f32[1024]{0:T(1024)} %param.13) | copy-start | bytes 12292
  509.0 141.1 %all-to-all-start.6 = ((f32[16,64,512]{2,1,0:T(8,128)}), f32[16,64,512]{2,1,0:T(8,128)}, u32[]{:S(2)}, u32[]{:S(2)}) async-start(f32[16,64,512]{2,1,0:T(8,128)} %bitcast.183), calls=%async_computation.6 | async-start | bytes 4194304 | tf_op jit(solution)/shard_map/all_to_all | solution.py:153
  520.4 2.2 copy-start.15
  522.6 2.9 copy-start.9
  525.6 1.4 copy-start.11
  525.6 2.0 copy-start.13
  530.8 3.1 collective-permute-start.1
  535.5 3.9 copy-start.3
  535.5 4.5 copy-start.5
  535.5 5.2 copy-start.10
  535.5 5.8 copy-start.12
  535.5 6.4 copy-start.14
where the time goes:
time: 661 us; the launch traced here: 654 us
  matrix products  236 us (36%)
  blocking collectives  140 us (21%)
  waiting for transfers between devices  102 us (15%)
  starting transfers between devices  70.1 us (11%)
  local copies, waits for them, and re-layouts  60.6 us (9%)
  other arithmetic  43.8 us (7%)
    psum x1, blocking collectives, on_device(): short_total, skip_total = lax.psum((short_part, skip_part), 'ctx')  81.7 us
    dot_general x5, matrix products, matmul_complex(): jnp.einsum(form, table_sin, data_real, precision=highest)  65.6 us
    all_to_all x1, blocking collectives, channel_correlate(): lax.all_to_all((result[1] * factor).reshape(flat_shape), 'ctx', split_axi...  58.5 us
    dot_general x5, matrix products, matmul_complex(): jnp.einsum(form, table_cos, data_real, precision=highest)  51.7 us
    dot_general x5, matrix products, matmul_complex(): jnp.einsum(form, table_sin, data_imag, precision=highest)  50.8 us
    dot_general x5, matrix products, matmul_complex(): jnp.einsum(form, table_cos, data_imag, precision=highest)  50.1 us
    all_to_all x1, waiting for transfers between devices, channel_correlate(): lax.all_to_all((result[0] * factor).reshape(flat_shape), 'ctx', split_axi...  37 us
    unnamed x49, local copies, waits for them, and re-layouts  34.4 us
  transfers between devices with their start and end apart: 8, of which 7 were waited for; matrix products, arithmetic and copies ran while one was open for 19% of the time, Pallas kernels for 0%

commit v1 on v0

--- a/solution.py
+++ b/solution.py
@@ -1,8 +1,12 @@
+import functools
 import math
 
 import jax
 import jax.numpy as jnp
+import numpy as np
 from jax import lax
+from jax.experimental import pallas as pl
+from jax.experimental.pallas import tpu as pltpu
 from jax.sharding import PartitionSpec as P
 
 highest = lax.Precision.HIGHEST
@@ -101,7 +105,7 @@
     return (returned[0], returned[1])
 
 
-def on_device(q_in, k_in, v_in, short_taps, long_filter, skip_gain, conv_saved, grad_out):
+def on_device_general(q_in, k_in, v_in, short_taps, long_filter, skip_gain, conv_saved, grad_out):
     local_rows = q_in.shape[0]
     slab_width = q_in.shape[1]
     ctx_count = lax.axis_size("ctx")
@@ -161,6 +165,637 @@
     return (grad_inputs[0], grad_inputs[1], grad_inputs[2], grad_filter, short_total, skip_total)
 
 
+MESH = pl.DeviceIdType.MESH
+LANES = 128
+HALF = 64
+N2 = 128
+MIB = 1 << 20
+
+
+def split_table(table):
+    high = table.astype(jnp.bfloat16)
+    low = (table - high.astype(np.float64)).astype(jnp.bfloat16)
+    return np.concatenate([high, high, low], axis=-1)
+
+
+def split_data(data):
+    high = data.astype(jnp.bfloat16)
+    low = (data - high.astype(jnp.float32)).astype(jnp.bfloat16)
+    return jnp.concatenate([high, low, high], axis=0)
+
+
+def dft_tables(seq_total):
+    n1_used = seq_total // 2 // N2
+    n1_total = 2 * n1_used
+    length = n1_total * N2
+    n1 = np.arange(n1_used)
+    k1 = np.arange(n1_total)
+    n2 = np.arange(N2)
+    turns = (n1[None, None, :] * k1[None, :, None] * N2 + n2[:, None, None] * k1[None, :, None]) % length
+    angle = 2.0 * np.pi / length * turns
+    cos, sin = np.cos(angle), np.sin(angle)
+    first = np.concatenate(
+        [np.concatenate([cos, sin], axis=2), np.concatenate([-sin, cos], axis=2)], axis=1
+    )
+    factor = 1.0 / (length * math.sqrt(seq_total))
+    cos_t, sin_t = np.swapaxes(cos, 1, 2) * factor, np.swapaxes(sin, 1, 2) * factor
+    last = np.concatenate(
+        [np.concatenate([cos_t, -sin_t], axis=2), np.concatenate([-sin_t, -cos_t], axis=2)], axis=1
+    )
+    inner = 2.0 * np.pi / N2 * ((n2[:, None] * n2[None, :]) % N2)
+    c, s = np.cos(inner), np.sin(inner)
+    second = np.block([[c, s], [-s, c]])
+    back = np.block([[c, -s], [s, c]])
+    odd = (np.arange(LANES) >= HALF)[None, :]
+    turn_k2 = (2.0 * np.pi / N2 * n2)[:, None]
+    turn_k1 = (2.0 * np.pi / length * k1)[:, None]
+    phase_k2 = np.concatenate(
+        [np.where(odd, np.cos(turn_k2), 1.0), np.where(odd, np.sin(turn_k2), 0.0)], axis=0
+    ).astype(np.float32)
+    phase_k1 = np.stack(
+        [np.where(odd, np.cos(turn_k1), 1.0), np.where(odd, np.sin(turn_k1), 0.0)], axis=1
+    ).astype(np.float32)
+    return (
+        split_table(first),
+        split_table(second),
+        split_table(back),
+        split_table(last),
+        phase_k2,
+        phase_k1,
+    )
+
+
+def low_lanes(shape):
+    return lax.broadcasted_iota(jnp.int32, shape, 1) < HALF
+
+
+def swap(value):
+    return pltpu.roll(value, HALF, 1)
+
+
+def fft_kernel(
+    f_ref, g_ref, k_ref, first_ref, second_ref, back_ref, last_ref, phase2_ref, phase1_ref,
+    corr_ref, zeta_ref, yf_ref, yg_ref, z_ref,
+):
+    n1_used = f_ref.shape[0] // N2
+    n1_total = 2 * n1_used
+    tail = corr_ref.shape[0] - f_ref.shape[0]
+    corr_ref[pl.ds(f_ref.shape[0], tail), :] = jnp.zeros((tail, LANES), jnp.float32)
+
+    def forward(n2, carry):
+        rows = pl.ds(n2, n1_used, stride=N2)
+        xg = g_ref[rows, :]
+        left = jnp.concatenate([f_ref[rows, :], k_ref[rows, :]], axis=0)
+        right = jnp.concatenate([xg, jnp.zeros_like(xg)], axis=0)
+        data = jnp.concatenate([left, right], axis=1)
+        out = jnp.dot(first_ref[n2], split_data(data), preferred_element_type=jnp.float32)
+        for part in range(2):
+            into = pl.ds(n2 + part * N2, n1_total, stride=2 * N2)
+            piece = out[part * n1_total : (part + 1) * n1_total]
+            yf_ref[into, :] = piece[:, :LANES]
+            yg_ref[into, :] = piece[:, LANES:]
+        return carry
+
+    lax.fori_loop(0, N2, forward, 0, unroll=4)
+
+    low = low_lanes((N2, LANES))
+
+    def product(k1):
+        rows = pl.ds(pl.multiple_of(k1 * 2 * N2, 2 * N2), 2 * N2)
+        data = jnp.concatenate([yf_ref[rows, :], yg_ref[rows, :]], axis=1)
+        out = jnp.dot(second_ref[...], split_data(data), preferred_element_type=jnp.float32)
+        fr, fi = out[:N2, :LANES], out[N2:, :LANES]
+        gr, gi = out[:N2, LANES:], out[N2:, LANES:]
+        sfr, sfi, sgr, sgi = swap(fr), swap(fi), swap(gr), swap(gi)
+        er, ei = jnp.where(low, fr, sfr), jnp.where(low, fi, sfi)
+        our, oui = jnp.where(low, sfr, fr), jnp.where(low, sfi, fi)
+        ar, ai = phase2_ref[:N2, :], phase2_ref[N2:, :]
+        both = phase1_ref[k1]
+        br, bi = both[0:1], both[1:2]
+        tr = ar * br - ai * bi
+        ti = ar * bi + ai * br
+        hr = tr * sgr - ti * sgi
+        hi = tr * sgi + ti * sgr
+        pr = er * gr + ei * gi + our * hr + oui * hi
+        pi = er * gi - ei * gr + our * hi - oui * hr
+        return jnp.concatenate([pr, pi], axis=0)
+
+    def middle(pair, carry):
+        k1 = pair * 2
+        data = jnp.concatenate([product(k1), product(k1 + 1)], axis=1)
+        out = jnp.dot(back_ref[...], split_data(data), preferred_element_type=jnp.float32)
+        for part in range(2):
+            for which in range(2):
+                into = pl.ds(part * n1_total + k1 + which, N2, stride=2 * n1_total)
+                z_ref[into, :] = out[
+                    part * N2 : (part + 1) * N2, which * LANES : (which + 1) * LANES
+                ]
+        return carry
+
+    lax.fori_loop(0, n1_total // 2, middle, 0)
+
+    def inverse(n2, carry):
+        rows = pl.ds(pl.multiple_of(n2 * 2 * n1_total, 2 * n1_total), 2 * n1_total)
+        out = jnp.dot(last_ref[n2], split_data(z_ref[rows, :]), preferred_element_type=jnp.float32)
+        into = pl.ds(n2, n1_used, stride=N2)
+        corr_ref[into, :] = out[:n1_used]
+        zeta_ref[into, :] = out[n1_used:]
+        return carry
+
+    lax.fori_loop(0, N2, inverse, 0, unroll=4)
+
+
+def meet_all(ctx_count, tp_count, me_c, me_t):
+    barrier = pltpu.get_barrier_semaphore()
+
+    def greet(index, carry):
+        c, t = index // tp_count, index % tp_count
+
+        @pl.when(jnp.logical_or(c != me_c, t != me_t))
+        def _():
+            pl.semaphore_signal(barrier, inc=1, device_id={"ctx": c, "tp": t}, device_id_type=MESH)
+
+        return carry
+
+    lax.fori_loop(0, ctx_count * tp_count, greet, 0)
+    pl.semaphore_wait(barrier, ctx_count * tp_count - 1)
+
+
+def column(block):
+    return pl.ds(pl.multiple_of(block * LANES, LANES), LANES)
+
+
+def extend(ext_ref, array_ref, before, after, cols):
+    rows = array_ref.shape[0]
+    ext_ref[0:8, :] = before
+    ext_ref[8 : 8 + rows, :] = array_ref[:, cols]
+    ext_ref[8 + rows : 16 + rows, :] = after
+
+
+def short_filter(ext_ref, taps_ref, branch, cols, count):
+    return (
+        taps_ref[branch, 0:1, cols] * ext_ref[8 : 8 + count, :]
+        + taps_ref[branch, 1:2, cols] * ext_ref[7 : 7 + count, :]
+        + taps_ref[branch, 2:3, cols] * ext_ref[6 : 6 + count, :]
+    )
+
+
+def long_gather(value_ref, taps_ref, branch, cols, count):
+    return (
+        taps_ref[branch, 0:1, cols] * value_ref[0:count, :]
+        + taps_ref[branch, 1:2, cols] * value_ref[1 : 1 + count, :]
+        + taps_ref[branch, 2:3, cols] * value_ref[2 : 2 + count, :]
+    )
+
+
+def tap_rows(value, ext_ref, count):
+    return [
+        jnp.sum(value * ext_ref[8 - o : 8 - o + count, :], axis=0, keepdims=True) for o in range(3)
+    ]
+
+
+def in_kernel(
+    ctx_count, tp_count,
+    q_ref, k_ref, v_ref, taps_ref, f_ref, saved_ref, out_grad_ref,
+    rf_ref, rg_ref, rk_ref, grad_q_ref, tap_q_ref, before_ref, after_ref,
+    pack_ref, ext_q, ext_k, ext_v, work, work2,
+    halo_send, halo_recv, send_sem, recv_sem, self_sem,
+):
+    me_c, me_t = lax.axis_index("ctx"), lax.axis_index("tp")
+    rows, width = q_ref.shape
+    blocks = width // LANES
+    half_rows = rows // 2
+    first_owner = me_t * (ctx_count // tp_count)
+    source_tp = me_c // (ctx_count // tp_count)
+    received = (rf_ref, rg_ref, rk_ref)
+    has_before, has_after = me_c > 0, me_c < ctx_count - 1
+    low = low_lanes((half_rows, LANES))
+    meet_all(ctx_count, tp_count, me_c, me_t)
+
+    forward = [
+        pltpu.make_async_remote_copy(
+            src_ref=ref.at[pl.ds(rows - 8, 8)],
+            dst_ref=before_ref.at[index],
+            send_sem=halo_send.at[index],
+            recv_sem=halo_recv.at[index],
+            device_id={"ctx": jnp.minimum(me_c + 1, ctx_count - 1), "tp": me_t},
+            device_id_type=MESH,
+        )
+        for index, ref in enumerate((q_ref, k_ref, v_ref))
+    ]
+    backward = [
+        pltpu.make_async_remote_copy(
+            src_ref=ref.at[pl.ds(0, 8)],
+            dst_ref=after_ref.at[index],
+            send_sem=halo_send.at[3 + index],
+            recv_sem=halo_recv.at[3 + index],
+            device_id={"ctx": jnp.maximum(me_c - 1, 0), "tp": me_t},
+            device_id_type=MESH,
+        )
+        for index, ref in enumerate((q_ref, k_ref, v_ref, out_grad_ref, saved_ref))
+    ]
+
+    @pl.when(has_after)
+    def _():
+        for copy in forward:
+            copy.start()
+
+    @pl.when(has_before)
+    def _():
+        for copy in backward:
+            copy.start()
+
+    @pl.when(jnp.logical_not(has_before))
+    def _():
+        before_ref[...] = jnp.zeros_like(before_ref)
+
+    @pl.when(jnp.logical_not(has_after))
+    def _():
+        after_ref[...] = jnp.zeros_like(after_ref)
+
+    def block_copy(array, owner_c, owner_t, block):
+        return pltpu.make_async_remote_copy(
+            src_ref=pack_ref.at[array, block],
+            dst_ref=received[array].at[pl.ds(pl.multiple_of(me_c * half_rows, half_rows), half_rows)],
+            send_sem=send_sem.at[array, block],
+            recv_sem=recv_sem.at[array, me_c],
+            device_id={"ctx": owner_c, "tp": owner_t},
+            device_id_type=MESH,
+        )
+
+    def self_copy(array, block):
+        return pltpu.make_async_copy(
+            pack_ref.at[array, block],
+            received[array].at[pl.ds(pl.multiple_of(me_c * half_rows, half_rows), half_rows)],
+            self_sem.at[array],
+        )
+
+    def is_self(owner_c, owner_t):
+        return jnp.logical_and(owner_c == me_c, owner_t == me_t)
+
+    def pack_and_send(array, column_block):
+        even = work[pl.ds(0, half_rows, stride=2), :]
+        odd = work[pl.ds(1, half_rows, stride=2), :]
+        pack_ref[array, 2 * column_block] = jnp.where(low, even, swap(odd))
+        pack_ref[array, 2 * column_block + 1] = jnp.where(low, swap(even), odd)
+        owner_c = first_owner + column_block
+        for owner_t in range(2):
+            block = 2 * column_block + owner_t
+            mine = is_self(owner_c, owner_t)
+
+            @pl.when(mine)
+            def _():
+                self_copy(array, block).start()
+
+            @pl.when(jnp.logical_not(mine))
+            def _():
+                block_copy(array, owner_c, owner_t, block).start()
+
+    def send_filter(column_block, carry):
+        work[0:rows, :] = f_ref[:, column(column_block)]
+        pack_and_send(0, column_block)
+        return carry
+
+    lax.fori_loop(0, blocks, send_filter, 0)
+
+    @pl.when(has_after)
+    def _():
+        for copy in forward:
+            copy.wait_send()
+        for copy in backward:
+            copy.wait_recv()
+
+    @pl.when(has_before)
+    def _():
+        for copy in forward:
+            copy.wait_recv()
+        for copy in backward:
+            copy.wait_send()
+
+    def send_grad(column_block, carry):
+        cols = column(column_block)
+        extend(ext_q, q_ref, before_ref[0, :, cols], after_ref[0, :, cols], cols)
+        work[0:rows, :] = out_grad_ref[:, cols] * short_filter(ext_q, taps_ref, 0, cols, rows)
+        pack_and_send(1, column_block)
+        return carry
+
+    lax.fori_loop(0, blocks, send_grad, 0)
+
+    def send_product(column_block, carry):
+        cols = column(column_block)
+        extend(ext_k, k_ref, before_ref[1, :, cols], after_ref[1, :, cols], cols)
+        extend(ext_v, v_ref, before_ref[2, :, cols], after_ref[2, :, cols], cols)
+        work[0:rows, :] = short_filter(ext_k, taps_ref, 1, cols, rows) * short_filter(
+            ext_v, taps_ref, 2, cols, rows
+        )
+        pack_and_send(2, column_block)
+        return carry
+
+    lax.fori_loop(0, blocks, send_product, 0)
+
+    def query(column_block, carry):
+        cols = column(column_block)
+        extend(ext_q, q_ref, before_ref[0, :, cols], after_ref[0, :, cols], cols)
+        here = out_grad_ref[:, cols] * saved_ref[:, cols]
+        work2[0:rows, :] = here
+        work2[rows : rows + 8, :] = after_ref[3, :, cols] * after_ref[4, :, cols]
+        grad_q_ref[:, cols] = long_gather(work2, taps_ref, 0, cols, rows)
+        sums = tap_rows(here, ext_q, rows)
+        tap_q_ref[:, cols] = jnp.concatenate(sums + [jnp.zeros((5, LANES), jnp.float32)], axis=0)
+        return carry
+
+    lax.fori_loop(0, blocks, query, 0)
+
+    for array in range(3):
+
+        def settle(index, carry):
+            owner_c, owner_t = first_owner + index // tp_count, index % tp_count
+            mine = is_self(owner_c, owner_t)
+
+            @pl.when(mine)
+            def _():
+                self_copy(array, index).wait()
+
+            @pl.when(jnp.logical_not(mine))
+            def _():
+                block_copy(array, owner_c, owner_t, index).wait_send()
+
+            @pl.when(jnp.logical_not(is_self(index, source_tp)))
+            def _():
+                pltpu.make_async_remote_copy(
+                    src_ref=pack_ref.at[array, index],
+                    dst_ref=received[array].at[
+                        pl.ds(pl.multiple_of(index * half_rows, half_rows), half_rows)
+                    ],
+                    send_sem=send_sem.at[array, index],
+                    recv_sem=recv_sem.at[array, index],
+                    device_id={"ctx": index, "tp": source_tp},
+                    device_id_type=MESH,
+                ).wait_recv()
+
+            return carry
+
+        lax.fori_loop(0, ctx_count, settle, 0)
+
+
+def out_kernel(
+    ctx_count, tp_count,
+    corr_ref, q_ref, k_ref, v_ref, out_grad_ref, taps_ref, skip_ref, tap_q_ref,
+    before_ref, after_ref,
+    grad_k_ref, grad_v_ref, total_ref,
+    arrived, ext_q, ext_k, ext_v, grad_w, k_short, v_short, work, gk, gv, part, parts, summed,
+    send_sem, recv_sem, self_sem, sum_send, sum_recv, spread_send, spread_recv,
+):
+    me_c, me_t = lax.axis_index("ctx"), lax.axis_index("tp")
+    rows, width = q_ref.shape
+    blocks = width // LANES
+    half_rows = rows // 2
+    more = half_rows + 8
+    longer = rows + 8
+    share = ctx_count // tp_count
+    source_tp = me_c // share
+    my_block = (me_c - source_tp * share) * tp_count + me_t
+    meet_all(ctx_count, tp_count, me_c, me_t)
+
+    def corr_rows(index):
+        return corr_ref.at[pl.ds(pl.multiple_of(index * half_rows, half_rows), more)]
+
+    def block_copy(index):
+        return pltpu.make_async_remote_copy(
+            src_ref=corr_rows(index),
+            dst_ref=arrived.at[my_block],
+            send_sem=send_sem.at[index],
+            recv_sem=recv_sem.at[my_block],
+            device_id={"ctx": index, "tp": source_tp},
+            device_id_type=MESH,
+        )
+
+    def self_copy():
+        return pltpu.make_async_copy(corr_rows(me_c), arrived.at[my_block], self_sem)
+
+    def is_self(c, t):
+        return jnp.logical_and(c == me_c, t == me_t)
+
+    def launch(index, carry):
+        mine = is_self(index, source_tp)
+
+        @pl.when(mine)
+        def _():
+            self_copy().start()
+
+        @pl.when(jnp.logical_not(mine))
+        def _():
+            block_copy(index).start()
+
+        return carry
+
+    lax.fori_loop(0, ctx_count, launch, 0)
+
+    def prepare(column_block, carry):
+        cols = column(column_block)
+        extend(ext_q, q_ref, before_ref[0, :, cols], after_ref[0, :, cols], cols)
+        extend(ext_k, k_ref, before_ref[1, :, cols], after_ref[1, :, cols], cols)
+        extend(ext_v, v_ref, before_ref[2, :, cols], after_ref[2, :, cols], cols)
+        q_short = short_filter(ext_q, taps_ref, 0, cols, longer)
+        grad_w[0:rows, cols] = out_grad_ref[:, cols] * q_short[:rows]
+        grad_w[rows:longer, cols] = after_ref[3, :, cols] * q_short[rows:]
+        k_short[:, cols] = short_filter(ext_k, taps_ref, 1, cols, longer)
+        v_short[:, cols] = short_filter(ext_v, taps_ref, 2, cols, longer)
+        return carry
+
+    lax.fori_loop(0, blocks, prepare, 0)
+
+    def settle(index, carry):
+        mine = is_self(index, source_tp)
+
+        @pl.when(mine)
+        def _():
+            self_copy().wait()
+
+        @pl.when(jnp.logical_not(mine))
+        def _():
+            block_copy(index).wait_send()
+
+        owner_c, owner_t = me_t * share + index // tp_count, index % tp_count
+
+        @pl.when(jnp.logical_not(is_self(owner_c, owner_t)))
+        def _():
+            pltpu.make_async_remote_copy(
+                src_ref=corr_rows(index),
+                dst_ref=arrived.at[index],
+                send_sem=send_sem.at[index],
+                recv_sem=recv_sem.at[index],
+                device_id={"ctx": owner_c, "tp": owner_t},
+                device_id_type=MESH,
+            ).wait_recv()
+
+        return carry
+
+    lax.fori_loop(0, ctx_count, settle, 0)
+    low = low_lanes((more, LANES))
+
+    def finish(column_block, carry):
+        cols = column(column_block)
+        one, two = arrived[2 * column_block], arrived[2 * column_block + 1]
+        work[pl.ds(0, more, stride=2), :] = jnp.where(low, one, swap(two))
+        work[pl.ds(1, more, stride=2), :] = jnp.where(low, swap(one), two)
+        extend(ext_k, k_ref, before_ref[1, :, cols], after_ref[1, :, cols], cols)
+        extend(ext_v, v_ref, before_ref[2, :, cols], after_ref[2, :, cols], cols)
+        weight, ks, vs = grad_w[:, cols], k_short[:, cols], v_short[:, cols]
+        grad_z = skip_ref[0:1, cols] * weight + work[0:longer, :]
+        gk[...] = grad_z * vs
+        gv[...] = grad_z * ks
+        grad_k_ref[:, cols] = long_gather(gk, taps_ref, 1, cols, rows)
+        grad_v_ref[:, cols] = long_gather(gv, taps_ref, 2, cols, rows)
+        sums = tap_rows(gk[0:rows, :], ext_k, rows) + tap_rows(gv[0:rows, :], ext_v, rows)
+        skip = jnp.sum((weight * (ks * vs))[:rows], axis=0, keepdims=True)
+        part[:, cols] = jnp.concatenate(
+            [tap_q_ref[0:3, cols]] + sums + [skip, jnp.zeros((6, LANES), jnp.float32)], axis=0
+        )
+        return carry
+
+    lax.fori_loop(0, blocks, finish, 0)
+
+    def piece(ref, index):
+        return ref.at[pl.ds(pl.multiple_of(index // blocks * 8, 8), 8), column(index % blocks)]
+
+    def sum_copy(index, slot):
+        return pltpu.make_async_remote_copy(
+            src_ref=piece(part, index),
+            dst_ref=parts.at[slot],
+            send_sem=sum_send.at[index],
+            recv_sem=sum_recv.at[slot],
+            device_id={"ctx": index, "tp": me_t},
+            device_id_type=MESH,
+        )
+
+    def spread_copy(index, slot):
+        return pltpu.make_async_remote_copy(
+            src_ref=summed,
+            dst_ref=piece(total_ref, slot),
+            send_sem=spread_send.at[index],
+            recv_sem=spread_recv.at[slot],
+            device_id={"ctx": index, "tp": me_t},
+            device_id_type=MESH,
+        )
+
+    def others(action):
+        def step(index, carry):
+            @pl.when(index != me_c)
+            def _():
+                action(index)
+
+            return carry
+
+        lax.fori_loop(0, ctx_count, step, 0)
+
+    others(lambda index: sum_copy(index, me_c).start())
+    parts[me_c] = part[
+        pl.ds(pl.multiple_of(me_c // blocks * 8, 8), 8), column(me_c % blocks)
+    ]
+
+    def sum_wait(index):
+        sum_copy(index, me_c).wait_send()
+        sum_copy(index, index).wait_recv()
+
+    others(sum_wait)
+    summed[...] = jnp.sum(parts[...], axis=0)
+    others(lambda index: spread_copy(index, me_c).start())
+    total_ref[pl.ds(pl.multiple_of(me_c // blocks * 8, 8), 8), column(me_c % blocks)] = summed[...]
+
+    def spread_wait(index):
+        spread_copy(index, me_c).wait_send()
+        spread_copy(index, index).wait_recv()
+
+    others(spread_wait)
+
+
+def on_device(q_in, k_in, v_in, short_taps, long_filter, skip_gain, conv_saved, grad_out):
+    rows, width = q_in.shape
+    ctx_count, tp_count = lax.axis_size("ctx"), lax.axis_size("tp")
+    group = width // ctx_count
+    seq_total = rows * ctx_count
+    fits = (
+        tp_count == 2
+        and group == HALF
+        and ctx_count % 2 == 0
+        and width == ctx_count // 2 * LANES
+        and rows % 256 == 0
+        and seq_total == 8192
+    )
+    if not fits:
+        return on_device_general(
+            q_in, k_in, v_in, short_taps, long_filter, skip_gain, conv_saved, grad_out
+        )
+    count = seq_total // 2
+    f32 = jnp.float32
+    vmem = pl.BlockSpec(memory_space=pltpu.VMEM)
+    anywhere = pl.BlockSpec(memory_space=pl.ANY)
+    shape = jax.ShapeDtypeStruct
+    packed = shape((count, LANES), f32)
+    dma = pltpu.SemaphoreType.DMA
+    ext = pltpu.VMEM((rows + 16, LANES), f32)
+    rf, rg, rk, grad_q, tap_q, before, after = pl.pallas_call(
+        functools.partial(in_kernel, ctx_count, tp_count),
+        out_shape=(
+            packed, packed, packed,
+            shape((rows, width), f32),
+            shape((8, width), f32),
+            shape((3, 8, width), f32),
+            shape((5, 8, width), f32),
+        ),
+        in_specs=[vmem] * 7,
+        out_specs=(anywhere, anywhere, anywhere, vmem, vmem, vmem, vmem),
+        scratch_shapes=[
+            pltpu.VMEM((3, ctx_count, rows // 2, LANES), f32),
+            ext, ext, ext, ext, ext,
+            dma((8,)), dma((8,)), dma((3, ctx_count)), dma((3, ctx_count)), dma((3,)),
+        ],
+        compiler_params=pltpu.CompilerParams(
+            collective_id=0, has_side_effects=True, vmem_limit_bytes=56 * MIB
+        ),
+        name="send_in",
+    )(q_in, k_in, v_in, short_taps, long_filter, conv_saved, grad_out)
+    tables = [jnp.asarray(table) for table in dft_tables(seq_total)]
+    corr, zeta = pl.pallas_call(
+        fft_kernel,
+        out_shape=(shape((count + 8, LANES), f32), packed),
+        in_specs=[vmem] * 9,
+        out_specs=(vmem, vmem),
+        scratch_shapes=[
+            pltpu.VMEM((2 * seq_total, LANES), f32),
+            pltpu.VMEM((2 * seq_total, LANES), f32),
+            pltpu.VMEM((2 * seq_total, LANES), f32),
+        ],
+        compiler_params=pltpu.CompilerParams(vmem_limit_bytes=60 * MIB),
+        name="correlate",
+    )(rf, rg, rk, *tables)
+    longer = pltpu.VMEM((rows + 8, width), f32)
+    grad_k, grad_v, total = pl.pallas_call(
+        functools.partial(out_kernel, ctx_count, tp_count),
+        out_shape=(shape((rows, width), f32), shape((rows, width), f32), shape((16, width), f32)),
+        in_specs=[anywhere] + [vmem] * 9,
+        out_specs=(vmem, vmem, vmem),
+        scratch_shapes=[
+            pltpu.VMEM((ctx_count, rows // 2 + 8, LANES), f32),
+            ext, ext, ext, longer, longer, longer, ext,
+            pltpu.VMEM((rows + 8, LANES), f32),
+            pltpu.VMEM((rows + 8, LANES), f32),
+            pltpu.VMEM((16, width), f32),
+            pltpu.VMEM((ctx_count, 8, LANES), f32),
+            pltpu.VMEM((8, LANES), f32),
+            dma((ctx_count,)), dma((ctx_count,)), dma(()),
+            dma((ctx_count,)), dma((ctx_count,)), dma((ctx_count,)), dma((ctx_count,)),
+        ],
+        compiler_params=pltpu.CompilerParams(
+            collective_id=1, has_side_effects=True, vmem_limit_bytes=56 * MIB
+        ),
+        name="send_back",
+    )(corr, q_in, k_in, v_in, grad_out, short_taps, skip_gain.reshape(1, width), tap_q, before, after)
+    grad_filter = jnp.transpose(zeta.reshape(seq_total, HALF))
+    return (grad_q, grad_k, grad_v, grad_filter, total[:9].reshape(3, 3, width), total[9])
+
+
 def solution(mesh):
     placed = (
         P("ctx", "tp"),

time: 661 us -> 480 us (0.73); the launches traced: 654 us -> 480 us
  Pallas kernels: 0 us -> 464 us
  matrix products: 236 us -> 0 us
  blocking collectives: 140 us -> 0 us
  waiting for transfers between devices: 102 us -> 0 us
  starting transfers between devices: 70.1 us -> 0 us
  local copies, waits for them, and re-layouts: 60.6 us -> 15.1 us
  other arithmetic: 43.8 us -> 0 us
    pallas_call x0 -> x3, Pallas kernels: none -> 464 us  [the longest x1 251 us: on_device(): pl.pallas_call(functools.partial(in_kernel, ctx_count, tp_count), out_sha...]
    dot_general x22 -> x0, matrix products: 236 us -> none  [the longest x5 65.6 us: matmul_complex(): jnp.einsum(form, table_sin, data_real, precision=highest)]
    all_to_all x6 -> x0, waiting for transfers between devices: 99.1 us -> none  [the longest x1 37 us: channel_correlate(): lax.all_to_all((result[0] * factor).reshape(flat_shape), 'ctx', split_axi...]
    psum x1 -> x0, blocking collectives: 81.7 us -> none  [on_device(): short_total, skip_total = lax.psum((short_part, skip_part), 'ctx')]
    all_to_all x6 -> x0, starting transfers between devices: 66.6 us -> none  [the longest x1 26.5 us: channel_correlate(): lax.all_to_all(filter_imag, 'ctx', split_axis=1, concat_axis=0, tiled=True)]
    all_to_all x1 -> x0, blocking collectives: 58.5 us -> none  [channel_correlate(): lax.all_to_all((result[1] * factor).reshape(flat_shape), 'ctx', split_axi...]
    unnamed x49 -> x12, local copies, waits for them, and re-layouts: 34.4 us -> 9.95 us
    reduce_sum x2 -> x0, other arithmetic: 19.2 us -> none  [the longest x1 12.6 us: on_device(): jnp.sum(grad_stack * extended[:, 2 - offset:2 - offset + local_rows], axi...]
  transfers between devices with their start and end apart: 8 -> 0, of which waited for: 7 -> 0; matrix products, arithmetic and copies ran while one was open for 19% -> 0% of each run, Pallas kernels for 0% -> 0%
where the time goes in v1:
time: 480 us
  Pallas kernels  464 us (97%)
  local copies, waits for them, and re-layouts  15.1 us (3%)
    pallas_call x1, Pallas kernels, on_device(): pl.pallas_call(functools.partial(in_kernel, ctx_count, tp_count), out_sha...  251 us
    pallas_call x1, Pallas kernels, on_device(): pl.pallas_call(functools.partial(out_kernel, ctx_count, tp_count), out_sh...  143 us
    pallas_call x1, Pallas kernels, on_device(): pl.pallas_call(fft_kernel, out_shape=(shape((count + 8, LANES), f32), pac...  70.4 us
    unnamed x12, local copies, waits for them, and re-layouts  9.95 us

profile of v1, /device:TPU:0, one launch (start us, length us, event | category | flops | bytes accessed | tf_op | source)
XLA Modules:
  0.0 479.9 jit_solution(7020783897278110895)
XLA Ops:
  0.6 250.7 %send_in.1 = (f32[4096,128]{1,0:T(8,128)}, f32[4096,128]{1,0:T(8,128)}, f32[4096,128]{1,0:T(8,128)}, f32[512,1024]{1,0:T(8,128)}, f32[8,1024]{1,0:T(8,128)}, /*i...) custom-call(f32[512,1024]{1,0:T(8,128)} %q_ref.3, f32[512,1024]{1,0:T(8,128)} %k_ref.3, f32[512,1024]{1,0:T(8,128)} %v_ref.3, ...), custom_call_target="tpu_custom_call" | custom-call | tf_op jit(solution)/shard_map/send_in/pallas_call | solution.py:738
  251.3 70.4 %correlate.1 = (f32[4104,128]{1,0:T(8,128)}, f32[4096,128]{1,0:T(8,128)}) custom-call(f32[4096,128]{1,0:T(8,128)} %get-tuple-element.19.f_ref, f32[4096,128]{1,0:T(8,128)} %get-tuple-element.20.g_ref, f32[4096,128]{1,0:T(8,128)} %get-tuple-element.21.k_ref, bf16[128,128,192]{2,1,0:T(8,128)(2,1)} %constant.12.clone.first_ref, ...), custom_call_target="tpu_custom_call" | custom-call | tf_op jit(solution)/shard_map/correlate/pallas_call | solution.py:760
  321.8 0.0 copy-start
  321.8 143.0 %send_back.1 = (f32[512,1024]{1,0:T(8,128)}, f32[512,1024]{1,0:T(8,128)}, f32[16,1024]{1,0:T(8,128)}) custom-call(f32[4104,128]{1,0:T(8,128)} %get-tuple-element.22.corr_ref, f32[512,1024]{1,0:T(8,128)} %q_ref.3, f32[512,1024]{1,0:T(8,128)} %k_ref.3, f32[512,1024]{1,0:T(8,128)} %v_ref.3, f32[512,1024]{1,0:T(8,128)} %out_grad_ref.3, f32[3,3,1024]{2,1,0:T(4,128)} %taps_ref.3, ...), custom_call_target="tpu_custom_call" | custom-call | tf_op jit(solution)/shard_map/send_back/pallas_call | solution.py:774
  464.8 1.4 slice.7
  466.2 1.5 reshape.23
  467.7 0.0 copy-done
  467.7 2.3 reshape.22
  469.9 0.0 copy-start.1
  470.0 3.9 copy.21
  473.9 0.0 copy-done.1
  473.9 0.0 copy-start.3
  473.9 1.3 copy.25
  475.2 1.0 copy-done.3
  476.2 0.0 copy-start.2
  476.2 1.3 copy.26
  477.6 1.0 copy-done.2
  478.6 1.3 copy.27
Async XLA Ops:
  321.8 145.9 %copy-start = (f32[4096,128]{1,0:T(8,128)S(1)}, f32[4096,128]{1,0:T(8,128)}, u32[]{:S(2)}) copy-start(f32[4096,128]{1,0:T(8,128)} %get-tuple-element.28) | copy-start | bytes 6291460
  469.9 3.9 copy-start.1
  473.9 2.3 copy-start.3
  476.2 2.3 copy-start.2
